TPU v7x, 128 devices: a whole 4x4x4 slice. The times are simulated.
128 devices in a mesh: outer: 32 (over z, y, core), grp: 4 (over x).
Axes of the slice: x: 4, y: 4, z: 4, core: 2. Of those that a mesh axis runs over, the one named last changes fastest.
Arguments:
- link_ids: int32 [98304, 8], P(('outer', 'grp')), may hold values from 0 to 98303, as said below
- path_states: bfloat16 [98304, 8, 128], P(('outer', 'grp')), may hold values from -1 to 1
- final_grad: bfloat16 [98304, 128], P(('outer', 'grp')), may hold values from -6 to 6
- link_states: bfloat16 [98304, 128], P(('outer', 'grp')), may hold values from -6 to 6
- agg_grad: bfloat16 [98304, 128], P(('outer', 'grp')), may hold values from -3 to 3
- w_in: bfloat16 [128, 384], replicated, may hold values from -0.5 to 0.5
- w_rec: bfloat16 [128, 384], replicated, may hold values from -0.5 to 0.5
- b_in: float32 [384], replicated, may hold values from -1 to 1
- b_rec: float32 [384], replicated, may hold values from -1 to 1
Outputs:
- path_grad: bfloat16 [98304, 128], P(('outer', 'grp'))
- link_grad: float32 [98304, 128], P(('outer', 'grp'))
- w_in_grad: float32 [128, 384], replicated
- w_rec_grad: float32 [128, 384], replicated
- b_in_grad: float32 [384], replicated
- b_rec_grad: float32 [384], replicated
Inputs may be any that keep to these rules, and one draw needn't show every extreme that they name: `link_ids`: within the 6144 hops of each device's paths (aligned blocks), at most 72 lie on links of any one owner (owner = id // 768), and exactly 72 for some owner in every block.
All inputs are finite; a program needn't handle non-finite values.
Results may differ from a plain program's by a relative error of at most 0.0035.
Values may be sent and summed in bfloat16 or wider, within the bound.
A program may use at most 128 MiB of HBM per device.

v0:
```python
import math
import jax
import jax.numpy as jnp
from jax import lax
from jax.sharding import PartitionSpec as P


def gru_backward(carry_grad, inputs, states, w_in, w_rec, b_in, b_rec):
    width = states.shape[-1]
    from_input = jnp.dot(inputs, w_in, preferred_element_type=jnp.float32) + b_in
    from_state = jnp.dot(states, w_rec, preferred_element_type=jnp.float32) + b_rec
    update_gate = jax.nn.sigmoid(from_input[:, :width] + from_state[:, :width])
    reset_gate = jax.nn.sigmoid(from_input[:, width : 2 * width] + from_state[:, width : 2 * width])
    recur_part = from_state[:, 2 * width :]
    candidate = jnp.tanh(from_input[:, 2 * width :] + reset_gate * recur_part)
    state_wide = states.astype(jnp.float32)
    cand_pre = carry_grad * (1.0 - update_gate) * (1.0 - candidate * candidate)
    update_pre = carry_grad * (state_wide - candidate) * update_gate * (1.0 - update_gate)
    reset_pre = cand_pre * recur_part * reset_gate * (1.0 - reset_gate)
    input_pre = jnp.concatenate([update_pre, reset_pre, cand_pre], axis=1).astype(jnp.bfloat16)
    state_pre = jnp.concatenate([update_pre, reset_pre, cand_pre * reset_gate], axis=1).astype(
        jnp.bfloat16
    )
    input_grad = jnp.dot(input_pre, w_in.T, preferred_element_type=jnp.float32)
    state_grad = carry_grad * update_gate + jnp.dot(
        state_pre, w_rec.T, preferred_element_type=jnp.float32
    )
    w_in_term = jnp.dot(inputs.T, input_pre, preferred_element_type=jnp.float32)
    w_rec_term = jnp.dot(states.T, state_pre, preferred_element_type=jnp.float32)
    b_in_term = jnp.sum(input_pre.astype(jnp.float32), axis=0)
    b_rec_term = jnp.sum(state_pre.astype(jnp.float32), axis=0)
    return (state_grad, input_grad, w_in_term, w_rec_term, b_in_term, b_rec_term)


def per_device(link_ids, path_states, final_grad, link_states, agg_grad, w_in, w_rec, b_in, b_rec):
    path_count, hop_count = link_ids.shape
    width = link_states.shape[1]
    row_count = path_count * hop_count
    devices = lax.axis_size(("outer", "grp"))
    capacity = 3 * row_count // (2 * devices)
    links_dev = link_states.shape[0]
    flat_ids = jnp.transpose(link_ids).reshape(row_count)
    owners = flat_ids // links_dev
    local_ids = flat_ids - owners * links_dev
    by_owner = jnp.argsort(owners, stable=True)
    sorted_owners = owners[by_owner]
    group_starts = jnp.searchsorted(
        sorted_owners, jnp.arange(devices, dtype=jnp.int32), side="left"
    )
    slot_sorted = (
        sorted_owners * capacity
        + jnp.arange(row_count, dtype=jnp.int32)
        - group_starts[sorted_owners]
    )
    slots = jnp.zeros((row_count,), jnp.int32).at[by_owner].set(slot_sorted)
    requests = jnp.full((devices * capacity,), links_dev, jnp.int32).at[slots].set(local_ids)
    requests = requests.reshape(devices, capacity)
    link_table = jnp.concatenate([link_states, agg_grad], axis=1)
    asked_ids = lax.all_to_all(requests, ("outer", "grp"), split_axis=0, concat_axis=0, tiled=True)
    clipped = jnp.minimum(asked_ids, links_dev - 1)
    returned = lax.all_to_all(
        link_table[clipped], ("outer", "grp"), split_axis=0, concat_axis=0, tiled=True
    )
    fetched = returned.reshape(devices * capacity, 2 * width)[slots].reshape(
        hop_count, path_count, 2 * width
    )
    carry_grad = final_grad.astype(jnp.float32)
    w_in_sum = jnp.zeros(w_in.shape, jnp.float32)
    w_rec_sum = jnp.zeros(w_rec.shape, jnp.float32)
    b_in_sum = jnp.zeros(b_in.shape, jnp.float32)
    b_rec_sum = jnp.zeros(b_rec.shape, jnp.float32)
    hop_grads = [None] * hop_count
    for hop in range(hop_count - 1, -1, -1):
        hop_rows = fetched[hop]
        carry_grad = carry_grad + hop_rows[:, width:].astype(jnp.float32)
        carry_grad, input_grad, w_in_term, w_rec_term, b_in_term, b_rec_term = gru_backward(
            carry_grad, hop_rows[:, :width], path_states[:, hop], w_in, w_rec, b_in, b_rec
        )
        hop_grads[hop] = input_grad
        w_in_sum = w_in_sum + w_in_term
        w_rec_sum = w_rec_sum + w_rec_term
        b_in_sum = b_in_sum + b_in_term
        b_rec_sum = b_rec_sum + b_rec_term
    grad_rows_all = jnp.stack(hop_grads, axis=0).reshape(row_count, width)
    outgoing = jnp.zeros((devices * capacity, width), jnp.float32).at[slots].set(grad_rows_all)
    incoming = lax.all_to_all(
        outgoing.reshape(devices, capacity, width).astype(jnp.bfloat16),
        ("outer", "grp"),
        split_axis=0,
        concat_axis=0,
        tiled=True,
    ).astype(jnp.float32)
    link_grad = (
        jnp.zeros((links_dev, width), jnp.float32)
        .at[asked_ids.reshape(-1)]
        .add(incoming.reshape(devices * capacity, width), mode="drop")
    )
    w_in_all, w_rec_all, b_in_all, b_rec_all = lax.psum(
        (w_in_sum, w_rec_sum, b_in_sum, b_rec_sum), ("outer", "grp")
    )
    norm_scale = 1.0 / math.sqrt(row_count * devices)
    return (
        carry_grad.astype(jnp.bfloat16),
        link_grad,
        w_in_all * norm_scale,
        w_rec_all * norm_scale,
        b_in_all * norm_scale,
        b_rec_all * norm_scale,
    )


def solution(mesh):
    placed = (
        P(("outer", "grp"), None),
        P(("outer", "grp"), None, None),
        P(("outer", "grp"), None),
        P(("outer", "grp"), None),
        P(("outer", "grp"), None),
        P(),
        P(),
        P(),
        P(),
    )
    return jax.shard_map(
        per_device,
        mesh=mesh,
        in_specs=placed,
        out_specs=(P(("outer", "grp"), None), P(("outer", "grp"), None), P(), P(), P(), P()),
        check_vma=False,
    )
```

profile of v0, /device:TPU:1, one launch (start us, length us, event | category | flops | bytes accessed | tf_op | source)
XLA Modules:
  0.0 602.4 jit_solution(14700198796793534372)
XLA Ops:
  8.0 6.7 %sort.17 = (s32[6144]{0:T(1024)}, s32[6144]{0:T(1024)S(1)}) sort(s32[6144]{0:T(1024)S(1)} %get-tuple-element.208, s32[6144]{0:T(1024)S(1)} %iota.10), dimensions={0}, to_apply=%region_0.1 | sort | flops 79872 | bytes 98304 | tf_op jit(solution)/shard_map/jit(argsort)/sort | solution.py:45
  14.8 34.3 %gather_fusion.1 = s32[6144]{0:T(1024)S(1)} fusion(s32[6144]{0:T(1024)S(1)} %get-tuple-element.208, s32[6144]{0:T(1024)S(1)} %get-tuple-element.209), kind=kCustom, calls=%fused_computation.1 | custom fusion | bytes 73728 | tf_op jit(solution)/shard_map/gather | solution.py:46
  49.1 15.8 %while.24 = (s32[]{:T(128)}, u32[128]{0:T(128)S(1)}, u32[128]{0:T(128)S(1)}, s32[6144]{0:T(1024)S(1)}, s32[]{:T(128)}, /*index=5*/s32[]{:T(128)}, s32[]{}) while((s32[]{:T(128)}, u32[128]{0:T(128)S(1)}, u32[128]{0:T(128)S(1)}, s32[6144]{0:T(1024)S(1)}, s32[]{:T(128)}, /*index=5*/s32[]{:T(128)}, s32[]{}) %tuple.107), condition=%wide.region_2.3_spmd.clone, body=%wide.region_1.2_spmd.clone.sunk | while | flops 2692 | bytes 10340 | solution.py:47
  65.0 36.8 %gather_fusion.2 = s32[6144]{0:T(1024)S(1)} fusion(s32[128]{0:T(128)S(1)} %convert_element_type.136, s32[6144]{0:T(1024)S(1)} %broadcast_clamp_fusion.2), kind=kCustom, calls=%fused_computation.2 | custom fusion | bytes 73728 | tf_op jit(solution)/shard_map/gather | solution.py:53
  101.8 23.0 %scatter_custom_fusion = s32[6144]{0:T(1024)S(1)} fusion(s32[6144]{0:T(1024)S(1)} %get-tuple-element.210, s32[6144]{0:T(1024)S(1)} %add_subtract_fusion, s32[]{:T(128)} %constant.53.clone.1), kind=kCustom, calls=%fused_computation.309 | custom fusion | bytes 24580 | tf_op jit(solution)/shard_map/scatter | solution.py:55
  125.4 23.0 %scatter_custom_fusion.1 = s32[9216]{0:T(1024)S(1)} fusion(s32[6144]{0:T(1024)S(1)} %get-tuple-element.206, s32[6144]{0:T(1024)S(1)} %get-tuple-element.207, s32[]{:T(128)} %constant.52.clone.1), kind=kCustom, calls=%fused_computation.304 | custom fusion | bytes 36868 | tf_op jit(solution)/shard_map/scatter | solution.py:56
  149.1 11.5 %all-to-all-start = ((s32[128,1,72]{2,1,0:T(1,128)}), s32[128,1,72]{2,1,0:T(1,128)S(1)}, u32[]{:S(2)}, u32[]{:S(2)}) async-start(s32[128,1,72]{2,1,0:T(1,128)} %bitcast.3), calls=%async_computation | async-start | bytes 131072 | tf_op jit(solution)/shard_map/all_to_all | solution.py:59
  160.7 9.5 %all-to-all-done = s32[128,1,72]{2,1,0:T(1,128)S(1)} async-done(((s32[128,1,72]{2,1,0:T(1,128)}), s32[128,1,72]{2,1,0:T(1,128)S(1)}, u32[]{:S(2)}, u32[]{:S(2)}) %all-to-all-start) | async-done | bytes 36896 | tf_op jit(solution)/shard_map/all_to_all | solution.py:59
  172.4 36.9 %gather_fusion.3 = bf16[9216,256]{1,0:T(8,128)(2,1)} fusion(bf16[768,256]{1,0:T(8,128)(2,1)S(1)} %pad_maximum_fusion.24, s32[9216]{0:T(1024)S(1)} %broadcast_clamp_fusion), kind=kCustom, calls=%fused_computation.3 | custom fusion | bytes 9474048 | tf_op jit(solution)/shard_map/gather | solution.py:62
  209.3 6.0 all-to-all-start.1
  215.3 3.3 fusion.154
  236.4 37.7 %all-to-all-done.1 = bf16[128,72,256]{2,1,0:T(8,128)(2,1)} async-done(((bf16[128,72,256]{2,1,0:T(8,128)(2,1)}), bf16[128,72,256]{2,1,0:T(8,128)(2,1)}, u32[]{:S(2)}, u32[]{:S(2)}) %all-to-all-start.1) | async-done | bytes 4718624 | tf_op jit(solution)/shard_map/all_to_all | solution.py:61
  274.1 25.2 %gather_fusion.4 = bf16[6144,256]{1,0:T(8,128)(2,1)S(1)} fusion(bf16[9216,256]{1,0:T(8,128)(2,1)} %bitcast.6, s32[6144]{0:T(1024)} %get-tuple-element.205), kind=kCustom, calls=%fused_computation.4 | custom fusion | bytes 6316032 | tf_op jit(solution)/shard_map/gather | solution.py:64
  311.9 1.7 copy.106
  313.6 1.7 copy.108
  315.3 1.8 copy.110
  317.1 1.8 copy.112
  318.8 1.7 copy.114
  320.6 1.7 copy.116
  322.3 1.7 copy.118
  324.1 1.7 copy.120
  325.8 2.1 fusion.137
  355.6 1.7 copy-done.120
  357.3 18.5 %scatter_custom_fusion.2 = f32[9216,128]{1,0:T(8,128)} fusion(s32[6144]{0:T(1024)} %copy-done.119, f32[6144,128]{1,0:T(8,128)} %bitcast.135, f32[]{:T(128)} %constant.64.clone.1), kind=kCustom, calls=%fused_computation.19 | custom fusion | bytes 4719104 | tf_op jit(solution)/shard_map/scatter | solution.py:85
  375.8 3.5 convert_element_type.154
  379.3 5.2 all-to-all-start.2
  384.6 1.7 copy.96
  391.3 1.6 convert_reduce_fusion.6
  395.5 74.0 %all-reduce = (f32[384]{0:T(512)S(1)}, f32[384]{0:T(512)S(1)}) all-reduce(f32[384]{0:T(512)S(1)} %get-tuple-element.221, f32[384]{0:T(512)S(1)} %get-tuple-element.220), channel_id=1, replica_groups=mesh['outer'=32,'grp'=4] {'outer','grp'}, use_global_device_ids=true, to_apply=%region_17.18 | all-reduce | flops 768 | bytes 6144 | tf_op jit(solution)/shard_map/psum | solution.py:98
  470.6 72.1 %all-reduce.4.cloned.1.call-done = (f32[128,384]{1,0:T(8,128)}, f32[128,384]{1,0:T(8,128)}) async-done(((f32[128,384]{1,0:T(8,128)}, f32[128,384]{1,0:T(8,128)}), (f32[128,384]{1,0:T(8,128)}, f32[128,384]{1,0:T(8,128)})) %all-reduce.4.cloned.1.call-update) | async-done | bytes 393232 | tf_op jit(solution)/shard_map/psum | solution.py:98
  542.8 1.8 broadcast_multiply_fusion
  544.6 50.7 %scatter_custom_fusion.3 = f32[768,128]{1,0:T(8,128)} fusion(s32[9216]{0:T(1024)} %bitcast.133, bf16[9216,128]{1,0:T(8,128)(2,1)} %bitcast.28, f32[]{:T(128)} %constant.64.clone.1), kind=kCustom, calls=%fused_computation.17 | custom fusion | flops 2359296 | bytes 2753024 | tf_op jit(solution)/shard_map/scatter-add | solution.py:96
  (392 shorter events, 85.1 us)
Async XLA Ops:
  7.2 293.4 %copy-start = (bf16[128,384]{1,0:T(8,128)(2,1)S(1)}, bf16[128,384]{1,0:T(8,128)(2,1)}, u32[]{:S(2)}) copy-start(bf16[128,384]{1,0:T(8,128)(2,1)} %param.16) | copy-start | bytes 294916
  64.9 95.7 %copy-start.99 = (bf16[768,128]{1,0:T(8,128)(2,1)S(1)}, bf16[768,128]{1,0:T(8,128)(2,1)}, u32[]{:S(2)}) copy-start(bf16[768,128]{1,0:T(8,128)(2,1)} %param.15) | copy-start | bytes 589828
  65.0 95.7 %copy-start.100 = (bf16[768,128]{1,0:T(8,128)(2,1)S(1)}, bf16[768,128]{1,0:T(8,128)(2,1)}, u32[]{:S(2)}) copy-start(bf16[768,128]{1,0:T(8,128)(2,1)} %param.14) | copy-start | bytes 589828
  125.4 23.7 %copy-start.119 = (s32[6144]{0:T(1024)}, s32[6144]{0:T(1024)S(1)}, u32[]{:S(2)}) copy-start(s32[6144]{0:T(1024)S(1)} %get-tuple-element.206) | copy-start | bytes 73732
  149.1 21.1 %all-to-all-start = ((s32[128,1,72]{2,1,0:T(1,128)}), s32[128,1,72]{2,1,0:T(1,128)S(1)}, u32[]{:S(2)}, u32[]{:S(2)}) async-start(s32[128,1,72]{2,1,0:T(1,128)} %bitcast.3), calls=%async_computation | async-start | bytes 131072 | tf_op jit(solution)/shard_map/all_to_all | solution.py:59
  209.3 64.8 %all-to-all-start.1 = ((bf16[128,72,256]{2,1,0:T(8,128)(2,1)}), bf16[128,72,256]{2,1,0:T(8,128)(2,1)}, u32[]{:S(2)}, u32[]{:S(2)}) async-start(bf16[128,72,256]{2,1,0:T(8,128)(2,1)} %bitcast.129), calls=%async_computation.1 | async-start | bytes 9437184 | tf_op jit(solution)/shard_map/all_to_all | solution.py:61
  223.7 7.7 %copy-start.24 = (bf16[768,1,128]{0,2,1:T(8,128)(2,1)}, bf16[768,1,128]{0,2,1:T(8,128)(2,1)S(1)}, u32[]{:S(2)}) copy-start(bf16[768,1,128]{0,2,1:T(8,128)(2,1)S(1)} %copy.117) | copy-start | bytes 589828
  224.1 8.7 %copy-start.22 = (bf16[768,1,128]{0,2,1:T(8,128)(2,1)}, bf16[768,1,128]{0,2,1:T(8,128)(2,1)S(1)}, u32[]{:S(2)}) copy-start(bf16[768,1,128]{0,2,1:T(8,128)(2,1)S(1)} %copy.119) | copy-start | bytes 589828
  224.5 9.8 %copy-start.20 = (bf16[768,1,128]{0,2,1:T(8,128)(2,1)}, bf16[768,1,128]{0,2,1:T(8,128)(2,1)S(1)}, u32[]{:S(2)}) copy-start(bf16[768,1,128]{0,2,1:T(8,128)(2,1)S(1)} %copy.121) | copy-start | bytes 589828
  327.9 27.3 %copy-start.38 = (bf16[768,128]{0,1:T(8,128)(2,1)}, bf16[768,128]{0,1:T(8,128)(2,1)S(1)}, u32[]{:S(2)}) copy-start(bf16[768,128]{0,1:T(8,128)(2,1)S(1)} %get-tuple-element.137) | copy-start | bytes 589828
  328.6 26.6 %copy-start.40 = (bf16[768,128]{0,1:T(8,128)(2,1)}, bf16[768,128]{0,1:T(8,128)(2,1)S(1)}, u32[]{:S(2)}) copy-start(bf16[768,128]{0,1:T(8,128)(2,1)S(1)} %get-tuple-element.193) | copy-start | bytes 589828
  328.6 26.6 %copy-start.42 = (bf16[768,128]{0,1:T(8,128)(2,1)}, bf16[768,128]{0,1:T(8,128)(2,1)S(1)}, u32[]{:S(2)}) copy-start(bf16[768,128]{0,1:T(8,128)(2,1)S(1)} %get-tuple-element.194) | copy-start | bytes 589828
  331.2 23.6 %copy-start.101 = (bf16[768,128]{0,1:T(8,128)(2,1)}, bf16[768,128]{0,1:T(8,128)(2,1)S(1)}, u32[]{:S(2)}) copy-start(bf16[768,128]{0,1:T(8,128)(2,1)S(1)} %get-tuple-element.140) | copy-start | bytes 589828
  331.5 23.3 %copy-start.46 = (bf16[768,128]{0,1:T(8,128)(2,1)}, bf16[768,128]{0,1:T(8,128)(2,1)S(1)}, u32[]{:S(2)}) copy-start(bf16[768,128]{0,1:T(8,128)(2,1)S(1)} %get-tuple-element.191) | copy-start | bytes 589828
  331.5 23.3 %copy-start.47 = (bf16[768,128]{0,1:T(8,128)(2,1)}, bf16[768,128]{0,1:T(8,128)(2,1)S(1)}, u32[]{:S(2)}) copy-start(bf16[768,128]{0,1:T(8,128)(2,1)S(1)} %get-tuple-element.192) | copy-start | bytes 589828
  333.6 20.7 %copy-start.102 = (bf16[768,128]{0,1:T(8,128)(2,1)}, bf16[768,128]{0,1:T(8,128)(2,1)S(1)}, u32[]{:S(2)}) copy-start(bf16[768,128]{0,1:T(8,128)(2,1)S(1)} %get-tuple-element.143) | copy-start | bytes 589828
  334.3 20.0 %copy-start.49 = (bf16[768,128]{0,1:T(8,128)(2,1)}, bf16[768,128]{0,1:T(8,128)(2,1)S(1)}, u32[]{:S(2)}) copy-start(bf16[768,128]{0,1:T(8,128)(2,1)S(1)} %get-tuple-element.189) | copy-start | bytes 589828
  334.3 20.0 %copy-start.51 = (bf16[768,128]{0,1:T(8,128)(2,1)}, bf16[768,128]{0,1:T(8,128)(2,1)S(1)}, u32[]{:S(2)}) copy-start(bf16[768,128]{0,1:T(8,128)(2,1)S(1)} %get-tuple-element.190) | copy-start | bytes 589828
  336.4 17.5 %copy-start.104 = (bf16[768,128]{0,1:T(8,128)(2,1)}, bf16[768,128]{0,1:T(8,128)(2,1)S(1)}, u32[]{:S(2)}) copy-start(bf16[768,128]{0,1:T(8,128)(2,1)S(1)} %get-tuple-element.146) | copy-start | bytes 589828
  337.1 16.8 %copy-start.55 = (bf16[768,128]{0,1:T(8,128)(2,1)}, bf16[768,128]{0,1:T(8,128)(2,1)S(1)}, u32[]{:S(2)}) copy-start(bf16[768,128]{0,1:T(8,128)(2,1)S(1)} %get-tuple-element.187) | copy-start | bytes 589828
  337.1 16.8 %copy-start.57 = (bf16[768,128]{0,1:T(8,128)(2,1)}, bf16[768,128]{0,1:T(8,128)(2,1)S(1)}, u32[]{:S(2)}) copy-start(bf16[768,128]{0,1:T(8,128)(2,1)S(1)} %get-tuple-element.188) | copy-start | bytes 589828
  339.2 14.3 %copy-start.106 = (bf16[768,128]{0,1:T(8,128)(2,1)}, bf16[768,128]{0,1:T(8,128)(2,1)S(1)}, u32[]{:S(2)}) copy-start(bf16[768,128]{0,1:T(8,128)(2,1)S(1)} %get-tuple-element.149) | copy-start | bytes 589828
  339.9 13.6 %copy-start.63 = (bf16[768,128]{0,1:T(8,128)(2,1)}, bf16[768,128]{0,1:T(8,128)(2,1)S(1)}, u32[]{:S(2)}) copy-start(bf16[768,128]{0,1:T(8,128)(2,1)S(1)} %get-tuple-element.186) | copy-start | bytes 589828
  339.9 46.4 %copy-start.61 = (bf16[768,128]{0,1:T(8,128)(2,1)}, bf16[768,128]{0,1:T(8,128)(2,1)S(1)}, u32[]{:S(2)}) copy-start(bf16[768,128]{0,1:T(8,128)(2,1)S(1)} %get-tuple-element.185) | copy-start | bytes 589828
  342.1 11.1 %copy-start.108 = (bf16[768,128]{0,1:T(8,128)(2,1)}, bf16[768,128]{0,1:T(8,128)(2,1)S(1)}, u32[]{:S(2)}) copy-start(bf16[768,128]{0,1:T(8,128)(2,1)S(1)} %get-tuple-element.152) | copy-start | bytes 589828
  342.7 10.4 %copy-start.67 = (bf16[768,128]{0,1:T(8,128)(2,1)}, bf16[768,128]{0,1:T(8,128)(2,1)S(1)}, u32[]{:S(2)}) copy-start(bf16[768,128]{0,1:T(8,128)(2,1)S(1)} %get-tuple-element.183) | copy-start | bytes 589828
  342.8 10.4 %copy-start.70 = (bf16[768,128]{0,1:T(8,128)(2,1)}, bf16[768,128]{0,1:T(8,128)(2,1)S(1)}, u32[]{:S(2)}) copy-start(bf16[768,128]{0,1:T(8,128)(2,1)S(1)} %get-tuple-element.184) | copy-start | bytes 589828
  344.9 7.9 %copy-start.111 = (bf16[768,128]{0,1:T(8,128)(2,1)}, bf16[768,128]{0,1:T(8,128)(2,1)S(1)}, u32[]{:S(2)}) copy-start(bf16[768,128]{0,1:T(8,128)(2,1)S(1)} %get-tuple-element.155) | copy-start | bytes 589828
  345.6 7.2 %copy-start.75 = (bf16[768,128]{0,1:T(8,128)(2,1)}, bf16[768,128]{0,1:T(8,128)(2,1)S(1)}, u32[]{:S(2)}) copy-start(bf16[768,128]{0,1:T(8,128)(2,1)S(1)} %get-tuple-element.181) | copy-start | bytes 589828
  345.6 7.2 %copy-start.78 = (bf16[768,128]{0,1:T(8,128)(2,1)}, bf16[768,128]{0,1:T(8,128)(2,1)S(1)}, u32[]{:S(2)}) copy-start(bf16[768,128]{0,1:T(8,128)(2,1)S(1)} %get-tuple-element.182) | copy-start | bytes 589828
  379.3 165.2 %all-to-all-start.2 = ((bf16[128,72,128]{2,1,0:T(8,128)(2,1)}), bf16[128,72,128]{2,1,0:T(8,128)(2,1)}, u32[]{:S(2)}, u32[]{:S(2)}) async-start(bf16[128,72,128]{2,1,0:T(8,128)(2,1)} %bitcast.130), calls=%async_computation.2 | async-start | bytes 4718592 | tf_op jit(solution)/shard_map/all_to_all | solution.py:86
  384.6 158.2 %all-reduce.4.cloned.1.call-start = ((), (), s32[]{:S(2)}) async-start(), calls=%async_computation.3 | async-start | bytes 786432 | tf_op jit(solution)/shard_map/psum | solution.py:98
  (93 other events, 171.8 us)
Sparse Core Ops, SparseCore 0:
  391.4 151.3 all-reduce.3
where the time goes:
time: 610 us; the launch traced here: 602 us
  local copies, waits for them, and re-layouts  257 us (42%)
  waiting for transfers between devices  119 us (20%)
  other arithmetic  74.6 us (12%)
  blocking collectives  74 us (12%)
  matrix products  38.7 us (6%)
  starting transfers between devices  22.7 us (4%)
  between operations  15.9 us (3%)
    psum x1, blocking collectives, per_device(): lax.psum((w_in_sum, w_rec_sum, b_in_sum, b_rec_sum), ('outer', 'grp'))  74 us
    psum x1, waiting for transfers between devices, per_device(): lax.psum((w_in_sum, w_rec_sum, b_in_sum, b_rec_sum), ('outer', 'grp'))  72.1 us
    scatter-add x1, other arithmetic, per_device(): link_grad = jnp.zeros((links_dev, width), jnp.float32).at[asked_ids.resha...  50.7 us
    all_to_all x1, waiting for transfers between devices, per_device(): lax.all_to_all(link_table[clipped], ('outer', 'grp'), split_axis=0, conca...  37.7 us
    unnamed x260, local copies, waits for them, and re-layouts  37.2 us
    gather x1, local copies, waits for them, and re-layouts, per_device(): link_table[clipped]  36.9 us
    gather x1, local copies, waits for them, and re-layouts, per_device(): group_starts[sorted_owners]  36.8 us
    gather x1, local copies, waits for them, and re-layouts, per_device(): sorted_owners = owners[by_owner]  34.3 us
  transfers between devices with their start and end apart: 4, of which 3 were waited for; matrix products, arithmetic and copies ran while one was open for 5% of the time, Pallas kernels for 0%

commit v1 on v0

--- a/solution.py
+++ b/solution.py
@@ -33,6 +33,11 @@
 
 
 def per_device(link_ids, path_states, final_grad, link_states, agg_grad, w_in, w_rec, b_in, b_rec):
+
+    def _read_modes(vec):
+        e_now = jax.lax.psum(vec, "grp")
+        return jax.lax.psum(e_now, "outer")
+
     path_count, hop_count = link_ids.shape
     width = link_states.shape[1]
     row_count = path_count * hop_count
@@ -95,8 +100,8 @@
         .at[asked_ids.reshape(-1)]
         .add(incoming.reshape(devices * capacity, width), mode="drop")
     )
-    w_in_all, w_rec_all, b_in_all, b_rec_all = lax.psum(
-        (w_in_sum, w_rec_sum, b_in_sum, b_rec_sum), ("outer", "grp")
+    w_in_all, w_rec_all, b_in_all, b_rec_all = _read_modes(
+        (w_in_sum, w_rec_sum, b_in_sum, b_rec_sum)
     )
     norm_scale = 1.0 / math.sqrt(row_count * devices)
     return (

time: 610 us -> 651 us (1.067)
  waiting for transfers between devices: 119 us -> 147 us
  blocking collectives: 74 us -> 86.1 us
    psum x1 -> x2, waiting for transfers between devices: 72.1 us -> 100 us  [the longest x1 100 us: _read_modes(): return jax.lax.psum(e_now, 'outer')]
    psum x1 -> x2, blocking collectives: 74 us -> 86.1 us  [the longest x1 64.1 us: _read_modes(): return jax.lax.psum(e_now, 'outer')]
  transfers between devices with their start and end apart: 4 -> 5, of which waited for: 3 -> 3; matrix products, arithmetic and copies ran while one was open for 5% -> 5% of each run, Pallas kernels for 0% -> 0%
where the time goes in v1:
time: 651 us; the launch traced here: 643 us
  local copies, waits for them, and re-layouts  257 us (39%)
  waiting for transfers between devices  147 us (23%)
  blocking collectives  86.1 us (13%)
  other arithmetic  74.6 us (11%)
  matrix products  38.7 us (6%)
  starting transfers between devices  22.8 us (4%)
  between operations  15.9 us (2%)
    psum x1, waiting for transfers between devices, _read_modes(): return jax.lax.psum(e_now, 'outer')  100 us
    psum x1, blocking collectives, _read_modes(): return jax.lax.psum(e_now, 'outer')  64.1 us
    scatter-add x1, other arithmetic, per_device(): link_grad = jnp.zeros((links_dev, width), jnp.float32).at[asked_ids.resha...  50.7 us
    all_to_all x1, waiting for transfers between devices, per_device(): lax.all_to_all(link_table[clipped], ('outer', 'grp'), split_axis=0, conca...  37.7 us
    unnamed x260, local copies, waits for them, and re-layouts  37.2 us
    gather x1, local copies, waits for them, and re-layouts, per_device(): link_table[clipped]  36.9 us
    gather x1, local copies, waits for them, and re-layouts, per_device(): group_starts[sorted_owners]  36.8 us
    gather x1, local copies, waits for them, and re-layouts, per_device(): sorted_owners = owners[by_owner]  34.3 us
  transfers between devices with their start and end apart: 5, of which 3 were waited for; matrix products, arithmetic and copies ran while one was open for 5% of the time, Pallas kernels for 0%

profile of v1, /device:TPU:1, one launch (start us, length us, event | category | flops | bytes accessed | tf_op | source)
XLA Modules:
  0.0 642.6 jit_solution(12628175410985241684)
XLA Ops:
  8.0 6.7 %sort.17 = (s32[6144]{0:T(1024)}, s32[6144]{0:T(1024)S(1)}) sort(s32[6144]{0:T(1024)S(1)} %get-tuple-element.212, s32[6144]{0:T(1024)S(1)} %iota.10), dimensions={0}, to_apply=%region_0.1 | sort | flops 79872 | bytes 98304 | tf_op jit(solution)/shard_map/jit(argsort)/sort | solution.py:50
  14.8 34.3 %gather_fusion.1 = s32[6144]{0:T(1024)S(1)} fusion(s32[6144]{0:T(1024)S(1)} %get-tuple-element.212, s32[6144]{0:T(1024)S(1)} %get-tuple-element.213), kind=kCustom, calls=%fused_computation.1 | custom fusion | bytes 73728 | tf_op jit(solution)/shard_map/gather | solution.py:51
  49.1 15.8 %while.24 = (s32[]{:T(128)}, u32[128]{0:T(128)S(1)}, u32[128]{0:T(128)S(1)}, s32[6144]{0:T(1024)S(1)}, s32[]{:T(128)}, /*index=5*/s32[]{:T(128)}, s32[]{}) while((s32[]{:T(128)}, u32[128]{0:T(128)S(1)}, u32[128]{0:T(128)S(1)}, s32[6144]{0:T(1024)S(1)}, s32[]{:T(128)}, /*index=5*/s32[]{:T(128)}, s32[]{}) %tuple.107), condition=%wide.region_2.3_spmd.clone, body=%wide.region_1.2_spmd.clone.sunk | while | flops 2692 | bytes 10340 | solution.py:52
  65.0 36.8 %gather_fusion.2 = s32[6144]{0:T(1024)S(1)} fusion(s32[128]{0:T(128)S(1)} %convert_element_type.136, s32[6144]{0:T(1024)S(1)} %broadcast_clamp_fusion.2), kind=kCustom, calls=%fused_computation.2 | custom fusion | bytes 73728 | tf_op jit(solution)/shard_map/gather | solution.py:58
  101.8 23.0 %scatter_custom_fusion = s32[6144]{0:T(1024)S(1)} fusion(s32[6144]{0:T(1024)S(1)} %get-tuple-element.214, s32[6144]{0:T(1024)S(1)} %add_subtract_fusion, s32[]{:T(128)} %constant.53.clone.1), kind=kCustom, calls=%fused_computation.309 | custom fusion | bytes 24580 | tf_op jit(solution)/shard_map/scatter | solution.py:60
  125.4 23.0 %scatter_custom_fusion.1 = s32[9216]{0:T(1024)S(1)} fusion(s32[6144]{0:T(1024)S(1)} %get-tuple-element.210, s32[6144]{0:T(1024)S(1)} %get-tuple-element.211, s32[]{:T(128)} %constant.52.clone.1), kind=kCustom, calls=%fused_computation.304 | custom fusion | bytes 36868 | tf_op jit(solution)/shard_map/scatter | solution.py:61
  149.1 11.5 %all-to-all-start = ((s32[128,1,72]{2,1,0:T(1,128)}), s32[128,1,72]{2,1,0:T(1,128)S(1)}, u32[]{:S(2)}, u32[]{:S(2)}) async-start(s32[128,1,72]{2,1,0:T(1,128)} %bitcast.3), calls=%async_computation | async-start | bytes 131072 | tf_op jit(solution)/shard_map/all_to_all | solution.py:64
  160.7 9.5 %all-to-all-done = s32[128,1,72]{2,1,0:T(1,128)S(1)} async-done(((s32[128,1,72]{2,1,0:T(1,128)}), s32[128,1,72]{2,1,0:T(1,128)S(1)}, u32[]{:S(2)}, u32[]{:S(2)}) %all-to-all-start) | async-done | bytes 36896 | tf_op jit(solution)/shard_map/all_to_all | solution.py:64
  172.4 36.9 %gather_fusion.3 = bf16[9216,256]{1,0:T(8,128)(2,1)} fusion(bf16[768,256]{1,0:T(8,128)(2,1)S(1)} %pad_maximum_fusion.24, s32[9216]{0:T(1024)S(1)} %broadcast_clamp_fusion), kind=kCustom, calls=%fused_computation.3 | custom fusion | bytes 9474048 | tf_op jit(solution)/shard_map/gather | solution.py:67
  209.3 6.0 all-to-all-start.1
  215.3 3.3 fusion.154
  236.4 37.7 %all-to-all-done.1 = bf16[128,72,256]{2,1,0:T(8,128)(2,1)} async-done(((bf16[128,72,256]{2,1,0:T(8,128)(2,1)}), bf16[128,72,256]{2,1,0:T(8,128)(2,1)}, u32[]{:S(2)}, u32[]{:S(2)}) %all-to-all-start.1) | async-done | bytes 4718624 | tf_op jit(solution)/shard_map/all_to_all | solution.py:66
  274.1 25.2 %gather_fusion.4 = bf16[6144,256]{1,0:T(8,128)(2,1)S(1)} fusion(bf16[9216,256]{1,0:T(8,128)(2,1)} %bitcast.6, s32[6144]{0:T(1024)} %get-tuple-element.209), kind=kCustom, calls=%fused_computation.4 | custom fusion | bytes 6316032 | tf_op jit(solution)/shard_map/gather | solution.py:69
  311.9 1.7 copy.106
  313.6 1.7 copy.108
  315.3 1.8 copy.110
  317.1 1.8 copy.112
  318.8 1.7 copy.114
  320.6 1.7 copy.116
  322.3 1.7 copy.118
  324.1 1.7 copy.120
  325.8 2.1 fusion.137
  355.6 1.7 copy-done.120
  357.3 18.5 %scatter_custom_fusion.2 = f32[9216,128]{1,0:T(8,128)} fusion(s32[6144]{0:T(1024)} %copy-done.119, f32[6144,128]{1,0:T(8,128)} %bitcast.135, f32[]{:T(128)} %constant.64.clone.1), kind=kCustom, calls=%fused_computation.19 | custom fusion | bytes 4719104 | tf_op jit(solution)/shard_map/scatter | solution.py:90
  375.8 3.5 convert_element_type.154
  379.3 5.2 all-to-all-start.2
  384.6 1.7 copy.96
  395.5 22.0 %all-reduce.2 = (f32[384]{0:T(512)S(1)}, f32[384]{0:T(512)S(1)}) all-reduce(f32[384]{0:T(512)S(1)} %get-tuple-element.225, f32[384]{0:T(512)S(1)} %get-tuple-element.224), channel_id=1, replica_groups=mesh['outer'=32,'grp'=4] {'grp'}, use_global_device_ids=true, to_apply=%region_19.20 | all-reduce | flops 768 | bytes 6144 | tf_op jit(solution)/shard_map/psum | solution.py:38
  417.6 64.1 %all-reduce = (f32[384]{0:T(512)S(1)}, f32[384]{0:T(512)S(1)}) all-reduce(f32[384]{0:T(512)S(1)} %get-tuple-element.137, f32[384]{0:T(512)S(1)} %get-tuple-element.138), channel_id=1, replica_groups=mesh['outer'=32,'grp'=4] {'outer'}, use_global_device_ids=true, to_apply=%region_20.21 | all-reduce | flops 768 | bytes 6144 | tf_op jit(solution)/shard_map/psum | solution.py:39
  482.9 100.1 %all-reduce.7.cloned.1.call-done = (f32[128,384]{1,0:T(8,128)}, f32[128,384]{1,0:T(8,128)}) async-done(((f32[128,384]{1,0:T(8,128)}, f32[128,384]{1,0:T(8,128)}), (f32[128,384]{1,0:T(8,128)}, f32[128,384]{1,0:T(8,128)})) %all-reduce.7.cloned.1.call-update) | async-done | bytes 393232 | tf_op jit(solution)/shard_map/psum | solution.py:39
  583.0 1.8 broadcast_multiply_fusion
  584.8 50.7 %scatter_custom_fusion.3 = f32[768,128]{1,0:T(8,128)} fusion(s32[9216]{0:T(1024)} %bitcast.133, bf16[9216,128]{1,0:T(8,128)(2,1)} %bitcast.28, f32[]{:T(128)} %constant.64.clone.1), kind=kCustom, calls=%fused_computation.17 | custom fusion | flops 2359296 | bytes 2753024 | tf_op jit(solution)/shard_map/scatter-add | solution.py:101
  (396 shorter events, 86.7 us)
Async XLA Ops:
  7.2 293.4 %copy-start = (bf16[128,384]{1,0:T(8,128)(2,1)S(1)}, bf16[128,384]{1,0:T(8,128)(2,1)}, u32[]{:S(2)}) copy-start(bf16[128,384]{1,0:T(8,128)(2,1)} %param.16) | copy-start | bytes 294916
  64.9 95.7 %copy-start.99 = (bf16[768,128]{1,0:T(8,128)(2,1)S(1)}, bf16[768,128]{1,0:T(8,128)(2,1)}, u32[]{:S(2)}) copy-start(bf16[768,128]{1,0:T(8,128)(2,1)} %param.15) | copy-start | bytes 589828
  65.0 95.7 %copy-start.100 = (bf16[768,128]{1,0:T(8,128)(2,1)S(1)}, bf16[768,128]{1,0:T(8,128)(2,1)}, u32[]{:S(2)}) copy-start(bf16[768,128]{1,0:T(8,128)(2,1)} %param.14) | copy-start | bytes 589828
  125.4 23.7 %copy-start.119 = (s32[6144]{0:T(1024)}, s32[6144]{0:T(1024)S(1)}, u32[]{:S(2)}) copy-start(s32[6144]{0:T(1024)S(1)} %get-tuple-element.210) | copy-start | bytes 73732
  149.1 21.1 %all-to-all-start = ((s32[128,1,72]{2,1,0:T(1,128)}), s32[128,1,72]{2,1,0:T(1,128)S(1)}, u32[]{:S(2)}, u32[]{:S(2)}) async-start(s32[128,1,72]{2,1,0:T(1,128)} %bitcast.3), calls=%async_computation | async-start | bytes 131072 | tf_op jit(solution)/shard_map/all_to_all | solution.py:64
  209.3 64.8 %all-to-all-start.1 = ((bf16[128,72,256]{2,1,0:T(8,128)(2,1)}), bf16[128,72,256]{2,1,0:T(8,128)(2,1)}, u32[]{:S(2)}, u32[]{:S(2)}) async-start(bf16[128,72,256]{2,1,0:T(8,128)(2,1)} %bitcast.129), calls=%async_computation.1 | async-start | bytes 9437184 | tf_op jit(solution)/shard_map/all_to_all | solution.py:66
  223.7 7.7 %copy-start.24 = (bf16[768,1,128]{0,2,1:T(8,128)(2,1)}, bf16[768,1,128]{0,2,1:T(8,128)(2,1)S(1)}, u32[]{:S(2)}) copy-start(bf16[768,1,128]{0,2,1:T(8,128)(2,1)S(1)} %copy.117) | copy-start | bytes 589828
  224.1 8.7 %copy-start.22 = (bf16[768,1,128]{0,2,1:T(8,128)(2,1)}, bf16[768,1,128]{0,2,1:T(8,128)(2,1)S(1)}, u32[]{:S(2)}) copy-start(bf16[768,1,128]{0,2,1:T(8,128)(2,1)S(1)} %copy.119) | copy-start | bytes 589828
  224.5 9.8 %copy-start.20 = (bf16[768,1,128]{0,2,1:T(8,128)(2,1)}, bf16[768,1,128]{0,2,1:T(8,128)(2,1)S(1)}, u32[]{:S(2)}) copy-start(bf16[768,1,128]{0,2,1:T(8,128)(2,1)S(1)} %copy.121) | copy-start | bytes 589828
  327.9 27.3 %copy-start.38 = (bf16[768,128]{0,1:T(8,128)(2,1)}, bf16[768,128]{0,1:T(8,128)(2,1)S(1)}, u32[]{:S(2)}) copy-start(bf16[768,128]{0,1:T(8,128)(2,1)S(1)} %get-tuple-element.141) | copy-start | bytes 589828
  328.6 26.6 %copy-start.40 = (bf16[768,128]{0,1:T(8,128)(2,1)}, bf16[768,128]{0,1:T(8,128)(2,1)S(1)}, u32[]{:S(2)}) copy-start(bf16[768,128]{0,1:T(8,128)(2,1)S(1)} %get-tuple-element.197) | copy-start | bytes 589828
  328.6 26.6 %copy-start.42 = (bf16[768,128]{0,1:T(8,128)(2,1)}, bf16[768,128]{0,1:T(8,128)(2,1)S(1)}, u32[]{:S(2)}) copy-start(bf16[768,128]{0,1:T(8,128)(2,1)S(1)} %get-tuple-element.198) | copy-start | bytes 589828
  331.2 23.6 %copy-start.101 = (bf16[768,128]{0,1:T(8,128)(2,1)}, bf16[768,128]{0,1:T(8,128)(2,1)S(1)}, u32[]{:S(2)}) copy-start(bf16[768,128]{0,1:T(8,128)(2,1)S(1)} %get-tuple-element.144) | copy-start | bytes 589828
  331.5 23.3 %copy-start.46 = (bf16[768,128]{0,1:T(8,128)(2,1)}, bf16[768,128]{0,1:T(8,128)(2,1)S(1)}, u32[]{:S(2)}) copy-start(bf16[768,128]{0,1:T(8,128)(2,1)S(1)} %get-tuple-element.195) | copy-start | bytes 589828
  331.5 23.3 %copy-start.47 = (bf16[768,128]{0,1:T(8,128)(2,1)}, bf16[768,128]{0,1:T(8,128)(2,1)S(1)}, u32[]{:S(2)}) copy-start(bf16[768,128]{0,1:T(8,128)(2,1)S(1)} %get-tuple-element.196) | copy-start | bytes 589828
  333.6 20.7 %copy-start.102 = (bf16[768,128]{0,1:T(8,128)(2,1)}, bf16[768,128]{0,1:T(8,128)(2,1)S(1)}, u32[]{:S(2)}) copy-start(bf16[768,128]{0,1:T(8,128)(2,1)S(1)} %get-tuple-element.147) | copy-start | bytes 589828
  334.3 20.0 %copy-start.49 = (bf16[768,128]{0,1:T(8,128)(2,1)}, bf16[768,128]{0,1:T(8,128)(2,1)S(1)}, u32[]{:S(2)}) copy-start(bf16[768,128]{0,1:T(8,128)(2,1)S(1)} %get-tuple-element.193) | copy-start | bytes 589828
  334.3 20.0 %copy-start.51 = (bf16[768,128]{0,1:T(8,128)(2,1)}, bf16[768,128]{0,1:T(8,128)(2,1)S(1)}, u32[]{:S(2)}) copy-start(bf16[768,128]{0,1:T(8,128)(2,1)S(1)} %get-tuple-element.194) | copy-start | bytes 589828
  336.4 17.5 %copy-start.104 = (bf16[768,128]{0,1:T(8,128)(2,1)}, bf16[768,128]{0,1:T(8,128)(2,1)S(1)}, u32[]{:S(2)}) copy-start(bf16[768,128]{0,1:T(8,128)(2,1)S(1)} %get-tuple-element.150) | copy-start | bytes 589828
  337.1 16.8 %copy-start.55 = (bf16[768,128]{0,1:T(8,128)(2,1)}, bf16[768,128]{0,1:T(8,128)(2,1)S(1)}, u32[]{:S(2)}) copy-start(bf16[768,128]{0,1:T(8,128)(2,1)S(1)} %get-tuple-element.191) | copy-start | bytes 589828
  337.1 16.8 %copy-start.57 = (bf16[768,128]{0,1:T(8,128)(2,1)}, bf16[768,128]{0,1:T(8,128)(2,1)S(1)}, u32[]{:S(2)}) copy-start(bf16[768,128]{0,1:T(8,128)(2,1)S(1)} %get-tuple-element.192) | copy-start | bytes 589828
  339.2 14.3 %copy-start.106 = (bf16[768,128]{0,1:T(8,128)(2,1)}, bf16[768,128]{0,1:T(8,128)(2,1)S(1)}, u32[]{:S(2)}) copy-start(bf16[768,128]{0,1:T(8,128)(2,1)S(1)} %get-tuple-element.153) | copy-start | bytes 589828
  339.9 13.6 %copy-start.63 = (bf16[768,128]{0,1:T(8,128)(2,1)}, bf16[768,128]{0,1:T(8,128)(2,1)S(1)}, u32[]{:S(2)}) copy-start(bf16[768,128]{0,1:T(8,128)(2,1)S(1)} %get-tuple-element.190) | copy-start | bytes 589828
  339.9 46.4 %copy-start.61 = (bf16[768,128]{0,1:T(8,128)(2,1)}, bf16[768,128]{0,1:T(8,128)(2,1)S(1)}, u32[]{:S(2)}) copy-start(bf16[768,128]{0,1:T(8,128)(2,1)S(1)} %get-tuple-element.189) | copy-start | bytes 589828
  342.1 11.1 %copy-start.108 = (bf16[768,128]{0,1:T(8,128)(2,1)}, bf16[768,128]{0,1:T(8,128)(2,1)S(1)}, u32[]{:S(2)}) copy-start(bf16[768,128]{0,1:T(8,128)(2,1)S(1)} %get-tuple-element.156) | copy-start | bytes 589828
  342.7 10.4 %copy-start.67 = (bf16[768,128]{0,1:T(8,128)(2,1)}, bf16[768,128]{0,1:T(8,128)(2,1)S(1)}, u32[]{:S(2)}) copy-start(bf16[768,128]{0,1:T(8,128)(2,1)S(1)} %get-tuple-element.187) | copy-start | bytes 589828
  342.8 10.4 %copy-start.70 = (bf16[768,128]{0,1:T(8,128)(2,1)}, bf16[768,128]{0,1:T(8,128)(2,1)S(1)}, u32[]{:S(2)}) copy-start(bf16[768,128]{0,1:T(8,128)(2,1)S(1)} %get-tuple-element.188) | copy-start | bytes 589828
  344.9 7.9 %copy-start.111 = (bf16[768,128]{0,1:T(8,128)(2,1)}, bf16[768,128]{0,1:T(8,128)(2,1)S(1)}, u32[]{:S(2)}) copy-start(bf16[768,128]{0,1:T(8,128)(2,1)S(1)} %get-tuple-element.159) | copy-start | bytes 589828
  345.6 7.2 %copy-start.75 = (bf16[768,128]{0,1:T(8,128)(2,1)}, bf16[768,128]{0,1:T(8,128)(2,1)S(1)}, u32[]{:S(2)}) copy-start(bf16[768,128]{0,1:T(8,128)(2,1)S(1)} %get-tuple-element.185) | copy-start | bytes 589828
  379.3 205.4 %all-to-all-start.2 = ((bf16[128,72,128]{2,1,0:T(8,128)(2,1)}), bf16[128,72,128]{2,1,0:T(8,128)(2,1)}, u32[]{:S(2)}, u32[]{:S(2)}) async-start(bf16[128,72,128]{2,1,0:T(8,128)(2,1)} %bitcast.130), calls=%async_computation.2 | async-start | bytes 4718592 | tf_op jit(solution)/shard_map/all_to_all | solution.py:91
  384.6 97.7 %all-reduce.9.cloned.1.call-start = ((), (), s32[]{:S(2)}) async-start(), calls=%async_computation.4 | async-start | bytes 786432 | tf_op jit(solution)/shard_map/psum | solution.py:38
  391.3 191.7 %all-reduce.7.cloned.1.call-start = ((), (), s32[]{:S(2)}) async-start(), calls=%async_computation.3 | async-start | bytes 786432 | tf_op jit(solution)/shard_map/psum | solution.py:39
  (94 other events, 179.8 us)
Sparse Core Ops, SparseCore 0:
  391.4 45.0 all-reduce.8
  482.4 100.5 all-reduce.6
